TPU v7x, 32 devices: a whole 2x2x4 slice. The times are simulated.
32 devices in a mesh: dp: 8 (over z, x), tensor: 4 (over y, core).
Axes of the slice: x: 2, y: 2, z: 4, core: 2. Of those that a mesh axis runs over, the one named last changes fastest.
Arguments:
- tokens: bfloat16 [2048, 8192], P('dp', 'tensor'), may hold values from -6 to 6
- key_value_weight: bfloat16 [8192, 8, 256], P('tensor'), may hold values from -0.09375 to 0.09375
- key_value_bias: bfloat16 [8, 256], P('tensor'), may hold values from -3 to 3
- adapter_down_weight: bfloat16 [16, 8192, 128], P('dp', 'tensor'), may hold values from -0.0625 to 0.0625
- adapter_up_weight: bfloat16 [16, 8, 2, 64, 128], P('dp', 'tensor'), may hold values from -0.75 to 0.75
- conversation_adapter: int32 [32], replicated, may hold values from 0 to 15, as said below
- adapter_slot_table: int32 [16], replicated, may hold values from 0 to 15, as said below
- span_length: int32 [32], P('dp'), may hold values from 40 to 64, as said below
- context_length: int32 [32], P('dp'), may hold values from 0 to 4096
Outputs:
- new_kv: bfloat16 [8, 2048, 256], P('tensor', 'dp')
Inputs may be any that keep to these rules, and one draw needn't show every extreme that they name: `conversation_adapter`: the 4 conversations of each index of dp use adapters whose slots lie on 4 different owners (owner of slot p: p // 2), so an owner serves at most one conversation of each index of dp, and some owner serves one of every index. `adapter_slot_table`: A permutation: every storage slot holds exactly one adapter. `span_length`: every index of dp has a conversation whose span fills all 64 slots.
All inputs are finite; a program needn't handle non-finite values.
Results may differ from a plain program's by a relative error of at most 0.019.
Values may be sent and summed in bfloat16 or wider, within the bound.
A program may use at most 128 MiB of HBM per device.

v0:
```python
import math

import jax
import jax.numpy as jnp
from jax import lax
from jax.sharding import PartitionSpec as P

rope_base = 1000000.0


def rotary(key_part, positions):
    half_dim = key_part.shape[-1] // 2
    inverse_freq = jnp.exp(
        jnp.arange(half_dim, dtype=jnp.float32) * (-2.0 * math.log(rope_base) / key_part.shape[-1])
    )
    angles = positions[:, None] * inverse_freq[None, :]
    angles = jnp.concatenate([angles, angles], axis=-1)
    turned = jnp.concatenate([-key_part[..., half_dim:], key_part[..., :half_dim]], axis=-1)
    return key_part * jnp.cos(angles) + turned * jnp.sin(angles)


def body(
    tokens,
    key_value_weight,
    key_value_bias,
    adapter_down_weight,
    adapter_up_weight,
    conversation_adapter,
    adapter_slot_table,
    span_length,
    context_length,
):
    dp_count = lax.axis_size("dp")
    owner_index = lax.axis_index("dp")
    conversation_present = span_length.shape[0]
    span_token_rows = tokens.shape[0] // conversation_present
    slice_width = tokens.shape[1]
    heads_present = key_value_bias.shape[0]
    head_span_width = key_value_bias.shape[1]
    head_dim = head_span_width // 2
    locally_stored = adapter_down_weight.shape[0]
    double_rank = adapter_down_weight.shape[2]
    adapter_ids = jnp.arange(adapter_slot_table.shape[0], dtype=jnp.int32)
    storage = jnp.sum(
        jnp.where(
            conversation_adapter[:, None] == adapter_ids[None, :], adapter_slot_table[None, :], 0
        ),
        axis=1,
    )
    owner_table = (storage // locally_stored).reshape(dp_count, conversation_present)
    local_table = (storage % locally_stored).reshape(dp_count, conversation_present)
    my_owners = lax.dynamic_slice_in_dim(owner_table, owner_index, 1, 0)[0]
    owner_ids = jnp.arange(dp_count, dtype=jnp.int32)
    routing = (my_owners[:, None] == owner_ids[None, :]).astype(jnp.bfloat16)
    served = owner_table == owner_index
    stored_ids = jnp.arange(locally_stored, dtype=jnp.int32)
    picked = served[:, :, None] & (local_table[:, :, None] == stored_ids[None, None, :])
    selector_f = jnp.sum(jnp.where(picked, 1.0, 0.0), axis=1).astype(jnp.float32)
    slot_chooser = selector_f.astype(jnp.bfloat16)
    conversation_rows = tokens.reshape(conversation_present, span_token_rows, slice_width)
    base_sum = lax.psum_scatter(
        jnp.einsum(
            "td,dhe->hte", tokens, key_value_weight, preferred_element_type=jnp.float32
        ).astype(jnp.bfloat16),
        "tensor",
        scatter_dimension=0,
        tiled=True,
    ).astype(jnp.float32)
    down_out = jnp.einsum(
        "fw,wqn->fqn", slot_chooser, adapter_down_weight, preferred_element_type=jnp.float32
    ).astype(jnp.bfloat16)
    up_out = jnp.einsum(
        "cp,ptdbi->ctdbi", slot_chooser, adapter_up_weight, preferred_element_type=jnp.float32
    ).astype(jnp.bfloat16)
    down_got, up_got = (
        lax.all_to_all(down_out, "dp", split_axis=0, concat_axis=0, tiled=True),
        lax.all_to_all(up_out, "dp", split_axis=0, concat_axis=0, tiled=True),
    )
    down_conv = jnp.einsum(
        "co,odk->cdk", routing, down_got, preferred_element_type=jnp.float32
    ).astype(jnp.bfloat16)
    up_conv = jnp.einsum(
        "co,ohgmf->chgmf", routing, up_got, preferred_element_type=jnp.float32
    ).astype(jnp.bfloat16)
    rank_part = jnp.einsum(
        "crd,cdk->crk", conversation_rows, down_conv, preferred_element_type=jnp.float32
    )
    rank_sum = lax.psum(rank_part.astype(jnp.bfloat16), "tensor")
    rank_halves = rank_sum.reshape(conversation_present, span_token_rows, 2, double_rank // 2)
    adapter_delta = jnp.einsum(
        "crgm,chgmf->crhgf", rank_halves, up_conv, preferred_element_type=jnp.float32
    ).astype(jnp.bfloat16)
    conversation_delta = adapter_delta.reshape(
        conversation_present, span_token_rows, heads_present * head_span_width
    ).astype(jnp.float32)
    delta_heads = jnp.transpose(
        conversation_delta.reshape(
            conversation_present * span_token_rows, heads_present, head_span_width
        ),
        (1, 0, 2),
    )
    projected = base_sum + key_value_bias.astype(jnp.float32)[:, None, :] + delta_heads
    positions = (
        (context_length[:, None] + jnp.arange(span_token_rows, dtype=jnp.int32)[None, :])
        .reshape(-1)
        .astype(jnp.float32)
    )
    rotated = rotary(projected[..., :head_dim], positions)
    live_mask = (
        jnp.arange(span_token_rows, dtype=jnp.int32)[None, :] < span_length[:, None]
    ).reshape(-1)
    joined = jnp.concatenate([rotated, projected[..., head_dim:]], axis=-1)
    return jnp.where(live_mask[None, :, None], joined, 0.0).astype(jnp.bfloat16)


def solution(mesh):
    placed = (
        P("dp", "tensor"),
        P("tensor", None, None),
        P("tensor", None),
        P("dp", "tensor", None),
        P("dp", "tensor", None, None, None),
        P(),
        P(),
        P("dp"),
        P("dp"),
    )
    return jax.shard_map(
        body, mesh=mesh, in_specs=placed, out_specs=P("tensor", "dp", None), check_vma=False
    )
```

profile of v0, /device:TPU:0, one launch (start us, length us, event | category | flops | bytes accessed | tf_op | source)
XLA Modules:
  0.0 193.4 jit_solution(5336113302605698851)
XLA Ops:
  6.5 0.8 select_reduce_fusion
  7.4 0.1 reduce_sum.21
  7.5 0.1 copy.31
  7.6 0.1 copy.32
  7.7 0.1 copy-done
  7.8 8.9 %convolution_convert_fusion = bf16[8,2048,128]{2,0,1:T(8,128)(2,1)S(1)} fusion(bf16[2,2048,128]{2,1,0:T(8,128)(2,1)S(1)} %copy-done, bf16[8,2]{0,1:T(2,128)(2,1)S(1)} %select_reduce_fusion.1), kind=kOutput, calls=%fused_computation.4 | convolution fusion | flops 10485760 | bytes 5242912 | tf_op jit(solution)/shard_map/fw,wqn->fqn/dot_general | solution.py:69
  16.7 2.7 %copy.37 = bf16[8,2048,128]{2,1,0:T(8,128)(2,1)} copy(bf16[8,2048,128]{2,0,1:T(8,128)(2,1)S(1)} %convolution_convert_fusion) | data formatting | bytes 8388608 | tf_op jit(solution)/shard_map/convert_element_type | solution.py:71
  19.4 7.3 %all-to-all-start.1 = ((bf16[8,2048,128]{2,1,0:T(8,128)(2,1)}), bf16[8,2048,128]{2,1,0:T(8,128)(2,1)}, u32[]{:S(2)}, u32[]{:S(2)}) async-start(bf16[8,2048,128]{2,1,0:T(8,128)(2,1)} %copy.37), calls=%async_computation.2 | async-start | bytes 8388608 | tf_op jit(solution)/shard_map/all_to_all | solution.py:76
  26.7 93.2 %all-to-all-done.1 = bf16[8,2048,128]{2,1,0:T(8,128)(2,1)} async-done(((bf16[8,2048,128]{2,1,0:T(8,128)(2,1)}), bf16[8,2048,128]{2,1,0:T(8,128)(2,1)}, u32[]{:S(2)}, u32[]{:S(2)}) %all-to-all-start.1) | async-done | bytes 4194336 | tf_op jit(solution)/shard_map/all_to_all | solution.py:76
  119.9 5.0 %fusion.6 = bf16[4,2048,128]{2,0,1:T(4,128)(2,1)S(1)} fusion(bf16[8,2048,128]{2,1,0:T(8,128)(2,1)} %all-to-all-done.1, s32[4]{0:T(128)S(1)} %dynamic-slice_bitcast_fusion), kind=kOutput, calls=%fused_computation.7 | convolution fusion | flops 17825824 | bytes 6291472 | tf_op jit(solution)/shard_map/co,odk->cdk/dot_general | solution.py:79
  124.9 0.5 fusion.20
  125.4 0.1 reshape.157
  125.5 0.7 copy.40
  126.3 0.2 reduce-scatter.2.cloned.1.call-start
  126.5 9.0 %fusion.12 = bf16[8,256,256]{1,2,0:T(8,128)(2,1)} fusion(bf16[2048,8,256]{2,1,0:T(8,128)(2,1)} %param.10, bf16[256,2048]{1,0:T(8,128)(2,1)S(1)} %copy-done.4), kind=kOutput, calls=%fused_computation.9 | convolution fusion | flops 2148007936 | bytes 10485760 | tf_op jit(solution)/shard_map/td,dhe->hte/dot_general | solution.py:62
  135.5 0.4 convolution_convert_fusion.1
  135.9 0.9 copy.34
  136.8 3.6 %all-to-all-start = ((bf16[8,2,2,64,128]{4,3,2,1,0:T(8,128)(2,1)}), bf16[8,2,2,64,128]{4,3,2,1,0:T(8,128)(2,1)S(1)}, u32[]{:S(2)}, u32[]{:S(2)}) async-start(bf16[8,2,2,64,128]{4,3,2,1,0:T(8,128)(2,1)} %copy.34), calls=%async_computation.1 | async-start | bytes 1048576 | tf_op jit(solution)/shard_map/all_to_all | solution.py:77
  140.6 0.1 convert_element_type.74
  140.7 0.1 lt.34
  140.8 0.1 broadcast_multiply_fusion
  140.9 0.5 fusion.30
  141.4 13.8 %all-to-all-done = bf16[8,2,2,64,128]{4,3,2,1,0:T(8,128)(2,1)S(1)} async-done(((bf16[8,2,2,64,128]{4,3,2,1,0:T(8,128)(2,1)}), bf16[8,2,2,64,128]{4,3,2,1,0:T(8,128)(2,1)S(1)}, u32[]{:S(2)}, u32[]{:S(2)}) %all-to-all-start) | async-done | bytes 524320 | tf_op jit(solution)/shard_map/all_to_all | solution.py:77
  155.1 0.4 convolution_convert_fusion.3
  155.6 1.3 all-reduce.2.cloned.1.call-done
  156.8 1.1 fusion.16
  158.0 0.4 copy.48
  158.4 0.6 reshape.165
  159.0 25.4 %reduce-scatter.2.cloned.1.call-done = bf16[2,256,256]{1,2,0:T(8,128)(2,1)} async-done(((bf16[8,256,256]{1,2,0:T(8,128)(2,1)}), bf16[2,256,256]{1,2,0:T(8,128)(2,1)}) %reduce-scatter.2.cloned.1.call-update) | async-done | bytes 262160 | tf_op jit(solution)/shard_map/reduce_scatter | solution.py:61
  184.4 1.1 bitcast_add_fusion
  185.6 0.1 fusion.27
  185.7 0.8 copy.44
  (24 shorter events, 0.4 us)
Async XLA Ops:
  6.5 1.3 copy-start
  19.4 100.5 %all-to-all-start.1 = ((bf16[8,2048,128]{2,1,0:T(8,128)(2,1)}), bf16[8,2048,128]{2,1,0:T(8,128)(2,1)}, u32[]{:S(2)}, u32[]{:S(2)}) async-start(bf16[8,2048,128]{2,1,0:T(8,128)(2,1)} %copy.37), calls=%async_computation.2 | async-start | bytes 8388608 | tf_op jit(solution)/shard_map/all_to_all | solution.py:76
  26.6 98.3 %copy-start.4 = (bf16[256,2048]{1,0:T(8,128)(2,1)S(1)}, bf16[256,2048]{1,0:T(8,128)(2,1)}, u32[]{:S(2)}) copy-start(bf16[256,2048]{1,0:T(8,128)(2,1)} %param.9) | copy-start | bytes 3145732
  26.6 130.2 %all-reduce.2.cloned.1.call-start = ((), (), s32[]{:S(2)}) async-start(), calls=%async_computation.4 | async-start | bytes 262144 | tf_op jit(solution)/shard_map/psum | solution.py:88
  126.2 9.3 %copy-start.1 = (bf16[2,2,2,64,128]{4,3,2,1,0:T(8,128)(2,1)S(1)}, bf16[2,2,2,64,128]{4,3,2,1,0:T(8,128)(2,1)}, u32[]{:S(2)}) copy-start(bf16[2,2,2,64,128]{4,3,2,1,0:T(8,128)(2,1)} %param.13) | copy-start | bytes 393220
  126.2 14.2 %copy-start.2 = (bf16[2,256]{1,0:T(2,128)(2,1)S(1)}, bf16[2,256]{1,0:T(2,128)(2,1)}, u32[]{:S(2)}) copy-start(bf16[2,256]{1,0:T(2,128)(2,1)} %param.11) | copy-start | bytes 3076
  126.2 14.2 %copy-start.3 = (s32[4]{0:T(128)S(1)}, s32[4]{0:T(128)}, u32[]{:S(2)}) copy-start(s32[4]{0:T(128)} %param.17) | copy-start | bytes 52
  126.2 14.4 %copy-start.5 = (s32[4]{0:T(128)S(1)}, s32[4]{0:T(128)}, u32[]{:S(2)}) copy-start(s32[4]{0:T(128)} %param.16) | copy-start | bytes 52
  126.3 58.2 %reduce-scatter.2.cloned.1.call-start = ((), (), s32[]{:S(2)}) async-start(), calls=%async_computation.3 | async-start | bytes 1310720 | tf_op jit(solution)/shard_map/reduce_scatter | solution.py:61
  136.8 18.3 %all-to-all-start = ((bf16[8,2,2,64,128]{4,3,2,1,0:T(8,128)(2,1)}), bf16[8,2,2,64,128]{4,3,2,1,0:T(8,128)(2,1)S(1)}, u32[]{:S(2)}, u32[]{:S(2)}) async-start(bf16[8,2,2,64,128]{4,3,2,1,0:T(8,128)(2,1)} %copy.34), calls=%async_computation.1 | async-start | bytes 1048576 | tf_op jit(solution)/shard_map/all_to_all | solution.py:77
Sparse Core Ops, SparseCore 0:
  126.3 30.4 all-reduce.1
  159.5 24.8 reduce-scatter.1
where the time goes:
time: 194 us; the launch traced here: 193 us
  waiting for transfers between devices  134 us (69%)
  matrix products  25.3 us (13%)
  between operations  13.6 us (7%)
  starting transfers between devices  11.2 us (6%)
  local copies, waits for them, and re-layouts  6.8 us (4%)
  other arithmetic  2.83 us (1%)
    all_to_all x1, waiting for transfers between devices, body(): lax.all_to_all(down_out, 'dp', split_axis=0, concat_axis=0, tiled=True)  93.2 us
    reduce_scatter x1, waiting for transfers between devices, body(): lax.psum_scatter(jnp.einsum('td,dhe->hte', tokens, key_value_weight, pref...  25.4 us
    all_to_all x1, waiting for transfers between devices, body(): lax.all_to_all(up_out, 'dp', split_axis=0, concat_axis=0, tiled=True)  13.8 us
    dot_general x1, matrix products, body(): jnp.einsum('td,dhe->hte', tokens, key_value_weight, preferred_element_typ...  9.01 us
    dot_general x1, matrix products, body(): jnp.einsum('fw,wqn->fqn', slot_chooser, adapter_down_weight, preferred_el...  8.9 us
    all_to_all x1, starting transfers between devices, body(): lax.all_to_all(down_out, 'dp', split_axis=0, concat_axis=0, tiled=True)  7.25 us
    dot_general x1, matrix products, body(): jnp.einsum('co,odk->cdk', routing, down_got, preferred_element_type=jnp.f...  4.98 us
  transfers between devices with their start and end apart: 4, of which 4 were waited for; matrix products, arithmetic and copies ran while one was open for 7% of the time, Pallas kernels for 0%

commit v1 on v0

--- a/solution.py
+++ b/solution.py
@@ -51,13 +51,14 @@
     local_table = (storage % locally_stored).reshape(dp_count, conversation_present)
     my_owners = lax.dynamic_slice_in_dim(owner_table, owner_index, 1, 0)[0]
     owner_ids = jnp.arange(dp_count, dtype=jnp.int32)
-    routing = (my_owners[:, None] == owner_ids[None, :]).astype(jnp.bfloat16)
-    served = owner_table == owner_index
-    stored_ids = jnp.arange(locally_stored, dtype=jnp.int32)
-    picked = served[:, :, None] & (local_table[:, :, None] == stored_ids[None, None, :])
-    selector_f = jnp.sum(jnp.where(picked, 1.0, 0.0), axis=1).astype(jnp.float32)
-    slot_chooser = selector_f.astype(jnp.bfloat16)
+    served_slot = jnp.sum(jnp.where(owner_table == owner_index, local_table, 0), axis=1)
     conversation_rows = tokens.reshape(conversation_present, span_token_rows, slice_width)
+    outgoing = jnp.zeros((dp_count, span_token_rows, slice_width), tokens.dtype)
+    for c in range(conversation_present):
+        outgoing = jnp.where(
+            (my_owners[c] == owner_ids)[:, None, None], conversation_rows[c][None], outgoing
+        )
+    visiting = lax.all_to_all(outgoing, "dp", split_axis=0, concat_axis=0, tiled=True)
     base_sum = lax.psum_scatter(
         jnp.einsum(
             "td,dhe->hte", tokens, key_value_weight, preferred_element_type=jnp.float32
@@ -66,30 +67,30 @@
         scatter_dimension=0,
         tiled=True,
     ).astype(jnp.float32)
-    down_out = jnp.einsum(
-        "fw,wqn->fqn", slot_chooser, adapter_down_weight, preferred_element_type=jnp.float32
+    rank_each = jnp.einsum(
+        "crd,sdk->scrk", visiting, adapter_down_weight, preferred_element_type=jnp.float32
+    )
+    rank_part = rank_each[0]
+    up_served = adapter_up_weight[0][None]
+    for s in range(1, locally_stored):
+        rank_part = jnp.where((served_slot == s)[:, None, None], rank_each[s], rank_part)
+        up_served = jnp.where(
+            (served_slot == s)[:, None, None, None, None], adapter_up_weight[s][None], up_served
+        )
+    rank_sum = lax.psum(rank_part.astype(jnp.bfloat16), "tensor")
+    rank_halves = rank_sum.reshape(dp_count, span_token_rows, 2, double_rank // 2)
+    served_delta = jnp.einsum(
+        "crgm,chgmf->crhgf", rank_halves, up_served, preferred_element_type=jnp.float32
     ).astype(jnp.bfloat16)
-    up_out = jnp.einsum(
-        "cp,ptdbi->ctdbi", slot_chooser, adapter_up_weight, preferred_element_type=jnp.float32
-    ).astype(jnp.bfloat16)
-    down_got, up_got = (
-        lax.all_to_all(down_out, "dp", split_axis=0, concat_axis=0, tiled=True),
-        lax.all_to_all(up_out, "dp", split_axis=0, concat_axis=0, tiled=True),
+    served_delta = served_delta.reshape(
+        dp_count, span_token_rows, heads_present * head_span_width
     )
-    down_conv = jnp.einsum(
-        "co,odk->cdk", routing, down_got, preferred_element_type=jnp.float32
-    ).astype(jnp.bfloat16)
-    up_conv = jnp.einsum(
-        "co,ohgmf->chgmf", routing, up_got, preferred_element_type=jnp.float32
-    ).astype(jnp.bfloat16)
-    rank_part = jnp.einsum(
-        "crd,cdk->crk", conversation_rows, down_conv, preferred_element_type=jnp.float32
-    )
-    rank_sum = lax.psum(rank_part.astype(jnp.bfloat16), "tensor")
-    rank_halves = rank_sum.reshape(conversation_present, span_token_rows, 2, double_rank // 2)
-    adapter_delta = jnp.einsum(
-        "crgm,chgmf->crhgf", rank_halves, up_conv, preferred_element_type=jnp.float32
-    ).astype(jnp.bfloat16)
+    returned = lax.all_to_all(served_delta, "dp", split_axis=0, concat_axis=0, tiled=True)
+    adapter_delta = jnp.zeros((conversation_present,) + returned.shape[1:], returned.dtype)
+    for o in range(dp_count):
+        adapter_delta = jnp.where(
+            (my_owners == o)[:, None, None], returned[o][None], adapter_delta
+        )
     conversation_delta = adapter_delta.reshape(
         conversation_present, span_token_rows, heads_present * head_span_width
     ).astype(jnp.float32)

time: 194 us -> 139 us (0.72)
  waiting for transfers between devices: 134 us -> 81.1 us
  matrix products: 25.3 us -> 11.3 us
  other arithmetic: 2.83 us -> 8.18 us
  local copies, waits for them, and re-layouts: 6.8 us -> 12 us
    all_to_all x2, waiting for transfers between devices: 107 us -> 55.6 us  [the longest x1 48.2 us: body(): lax.all_to_all(outgoing, 'dp', split_axis=0, concat_axis=0, tiled=True)]
    reduce_scatter x1, waiting for transfers between devices: 25.4 us -> 3.6 us  [body(): lax.psum_scatter(jnp.einsum('td,dhe->hte', tokens, key_value_weight, pref...]
    psum x1, waiting for transfers between devices: 1.28 us -> 21.9 us  [body(): rank_sum = lax.psum(rank_part.astype(jnp.bfloat16), 'tensor')]
    dot_general x6 -> x2, matrix products: 16.3 us -> 2.04 us  [the longest x1 1.33 us: body(): jnp.einsum('crgm,chgmf->crhgf', rank_halves, up_served, preferred_element...]
    broadcast_in_dim x0 -> x42, local copies, waits for them, and re-layouts: none -> 6.52 us  [the longest x41 6.51 us: body(): jnp.where((my_owners == o)[:, None, None], returned[o][None], adapter_delta)]
    convert_element_type x2 -> x1, local copies, waits for them, and re-layouts: 3.59 us -> 0.54 us  [body(): served_delta = jnp.einsum('crgm,chgmf->crhgf', rank_halves, up_served, pr...]
    eq x1 -> x5, other arithmetic: 0.01 us -> 2.55 us  [the longest x2 2.52 us: body(): my_owners[c] == owner_ids]
    select_n x1 -> x2, other arithmetic: 0.01 us -> 2.05 us  [the longest x1 1.92 us: body(): jnp.where((my_owners[c] == owner_ids)[:, None, None], conversation_rows[c...]
  transfers between devices with their start and end apart: 4 -> 4, of which waited for: 4 -> 4; matrix products, arithmetic and copies ran while one was open for 7% -> 15% of each run, Pallas kernels for 0% -> 0%
where the time goes in v1:
time: 139 us
  waiting for transfers between devices  81.1 us (58%)
  between operations  13.7 us (10%)
  starting transfers between devices  12.9 us (9%)
  local copies, waits for them, and re-layouts  12 us (9%)
  matrix products  11.3 us (8%)
  other arithmetic  8.18 us (6%)
    all_to_all x1, waiting for transfers between devices, body(): lax.all_to_all(outgoing, 'dp', split_axis=0, concat_axis=0, tiled=True)  48.2 us
    psum x1, waiting for transfers between devices, body(): rank_sum = lax.psum(rank_part.astype(jnp.bfloat16), 'tensor')  21.9 us
    dot_general x1, matrix products, body(): jnp.einsum('td,dhe->hte', tokens, key_value_weight, preferred_element_typ...  9.23 us
    all_to_all x1, waiting for transfers between devices, body(): lax.all_to_all(served_delta, 'dp', split_axis=0, concat_axis=0, tiled=True)  7.39 us
    all_to_all x1, starting transfers between devices, body(): lax.all_to_all(outgoing, 'dp', split_axis=0, concat_axis=0, tiled=True)  7.25 us
    broadcast_in_dim x41, local copies, waits for them, and re-layouts, body(): jnp.where((my_owners == o)[:, None, None], returned[o][None], adapter_delta)  6.51 us
    all_to_all x1, starting transfers between devices, body(): lax.all_to_all(served_delta, 'dp', split_axis=0, concat_axis=0, tiled=True)  5.52 us
    reduce_scatter x1, waiting for transfers between devices, body(): lax.psum_scatter(jnp.einsum('td,dhe->hte', tokens, key_value_weight, pref...  3.6 us
  transfers between devices with their start and end apart: 4, of which 4 were waited for; matrix products, arithmetic and copies ran while one was open for 15% of the time, Pallas kernels for 0%

profile of v1, /device:TPU:0, one launch (start us, length us, event | category | flops | bytes accessed | tf_op | source)
XLA Modules:
  0.0 139.1 jit_solution(17579780869747470158)
XLA Ops:
  6.5 0.8 select_reduce_fusion
  7.6 0.7 fusion.32
  8.3 1.3 fusion.31
  9.5 1.2 iota_compare_fusion.2
  10.7 1.3 iota_compare_fusion.4
  12.1 1.9 %select_select_fusion = bf16[8,64,2048]{2,1,0:T(8,128)(2,1)} fusion(pred[8]{0:T(512)(128)(4,1)S(1)} %get-tuple-element.40, pred[8]{0:T(512)(128)(4,1)S(1)} %get-tuple-element.41, pred[8]{0:T(512)(128)(4,1)S(1)} %get-tuple-element.42, pred[8]{0:T(512)(128)(4,1)S(1)} %get-tuple-element.43, bf16[64,2048]{1,0:T(8,128)(2,1)S(1)} %get-tuple-element.9, ...), kind=kLoop, calls=%fused_computation.4 | loop fusion | flops 4194304 | bytes 3145760 | tf_op jit(solution)/shard_map/jit(_where)/select_n | solution.py:58
  14.0 7.3 %all-to-all-start = ((bf16[8,64,2048]{2,1,0:T(8,128)(2,1)}), bf16[8,64,2048]{2,1,0:T(8,128)(2,1)S(1)}, u32[]{:S(2)}, u32[]{:S(2)}) async-start(bf16[8,64,2048]{2,1,0:T(8,128)(2,1)} %select_select_fusion), calls=%async_computation.1 | async-start | bytes 4194304 | tf_op jit(solution)/shard_map/all_to_all | solution.py:61
  21.3 48.2 %all-to-all-done = bf16[8,64,2048]{2,1,0:T(8,128)(2,1)S(1)} async-done(((bf16[8,64,2048]{2,1,0:T(8,128)(2,1)}), bf16[8,64,2048]{2,1,0:T(8,128)(2,1)S(1)}, u32[]{:S(2)}, u32[]{:S(2)}) %all-to-all-start) | async-done | bytes 2097184 | tf_op jit(solution)/shard_map/all_to_all | solution.py:61
  69.5 0.7 fusion.11
  70.4 0.8 copy.35
  71.3 9.2 %fusion.7 = bf16[8,256,256]{1,2,0:T(8,128)(2,1)} fusion(bf16[2048,8,256]{2,1,0:T(8,128)(2,1)} %param.10, bf16[256,2048]{1,0:T(8,128)(2,1)} %param.9), kind=kOutput, calls=%fused_computation.6 | convolution fusion | flops 2148007936 | bytes 10485760 | tf_op jit(solution)/shard_map/td,dhe->hte/dot_general | solution.py:63
  80.6 21.9 %all-reduce.2.cloned.1.call-done = bf16[8,64,2,64]{3,1,2,0:T(8,128)(2,1)} async-done(((bf16[8,64,2,64]{3,1,2,0:T(8,128)(2,1)}), bf16[8,64,2,64]{3,1,2,0:T(8,128)(2,1)}) %all-reduce.2.cloned.1.call-update) | async-done | bytes 131088 | tf_op jit(solution)/shard_map/psum | solution.py:80
  102.4 1.3 fusion.10
  103.8 0.5 copy.36
  104.3 1.0 reshape.215
  105.3 5.5 %all-to-all-start.1 = ((bf16[8,64,512]{2,1,0:T(8,128)(2,1)}), bf16[8,64,512]{2,1,0:T(8,128)(2,1)S(1)}, u32[]{:S(2)}, u32[]{:S(2)}) async-start(bf16[8,64,512]{2,1,0:T(8,128)(2,1)} %reshape.215), calls=%async_computation.2 | async-start | bytes 1048576 | tf_op jit(solution)/shard_map/all_to_all | solution.py:88
  111.3 0.6 broadcast_in_dim.327
  112.0 0.7 broadcast_in_dim.333
  112.7 0.6 broadcast_in_dim.339
  113.3 0.6 broadcast_in_dim.345
  114.0 0.6 broadcast_in_dim.351
  114.7 0.6 broadcast_in_dim.294
  115.7 1.1 fusion.26
  116.8 7.4 %all-to-all-done.1 = bf16[8,64,512]{2,1,0:T(8,128)(2,1)S(1)} async-done(((bf16[8,64,512]{2,1,0:T(8,128)(2,1)}), bf16[8,64,512]{2,1,0:T(8,128)(2,1)S(1)}, u32[]{:S(2)}, u32[]{:S(2)}) %all-to-all-start.1) | async-done | bytes 524320 | tf_op jit(solution)/shard_map/all_to_all | solution.py:88
  124.4 0.2 copy.37
  124.6 0.2 copy.38
  124.9 0.2 copy.39
  125.5 0.2 copy.41
  126.3 0.2 copy.44
  126.5 3.6 %reduce-scatter.2.cloned.1.call-done = bf16[2,256,256]{1,2,0:T(8,128)(2,1)} async-done(((bf16[8,256,256]{1,2,0:T(8,128)(2,1)}), bf16[2,256,256]{1,2,0:T(8,128)(2,1)}) %reduce-scatter.2.cloned.1.call-update) | async-done | bytes 262160 | tf_op jit(solution)/shard_map/reduce_scatter | solution.py:62
  130.1 1.2 bitcast_add_fusion
  131.4 0.8 copy.45
  (64 shorter events, 3.1 us)
Async XLA Ops:
  6.5 62.9 %copy-start = (bf16[2,2048,128]{2,1,0:T(8,128)(2,1)S(1)}, bf16[2,2048,128]{2,1,0:T(8,128)(2,1)}, u32[]{:S(2)}) copy-start(bf16[2,2048,128]{2,1,0:T(8,128)(2,1)} %param.12) | copy-start | bytes 3145732
  14.0 55.5 %all-to-all-start = ((bf16[8,64,2048]{2,1,0:T(8,128)(2,1)}), bf16[8,64,2048]{2,1,0:T(8,128)(2,1)S(1)}, u32[]{:S(2)}, u32[]{:S(2)}) async-start(bf16[8,64,2048]{2,1,0:T(8,128)(2,1)} %select_select_fusion), calls=%async_computation.1 | async-start | bytes 4194304 | tf_op jit(solution)/shard_map/all_to_all | solution.py:61
  21.2 81.2 %all-reduce.2.cloned.1.call-start = ((), (), s32[]{:S(2)}) async-start(), calls=%async_computation.4 | async-start | bytes 524288 | tf_op jit(solution)/shard_map/psum | solution.py:80
  71.2 9.3 %copy-start.2 = (bf16[2,2,2,64,128]{4,3,2,1,0:T(8,128)(2,1)S(1)}, bf16[2,2,2,64,128]{4,3,2,1,0:T(8,128)(2,1)}, u32[]{:S(2)}) copy-start(bf16[2,2,2,64,128]{4,3,2,1,0:T(8,128)(2,1)} %param.13) | copy-start | bytes 393220
  71.2 58.9 %reduce-scatter.2.cloned.1.call-start = ((), (), s32[]{:S(2)}) async-start(), calls=%async_computation.3 | async-start | bytes 1310720 | tf_op jit(solution)/shard_map/reduce_scatter | solution.py:62
  102.4 12.9 %copy-start.3 = (bf16[2,256]{1,0:T(2,128)(2,1)S(1)}, bf16[2,256]{1,0:T(2,128)(2,1)}, u32[]{:S(2)}) copy-start(bf16[2,256]{1,0:T(2,128)(2,1)} %param.11) | copy-start | bytes 3076
  102.4 12.9 %copy-start.4 = (s32[4]{0:T(128)S(1)}, s32[4]{0:T(128)}, u32[]{:S(2)}) copy-start(s32[4]{0:T(128)} %param.17) | copy-start | bytes 52
  102.4 13.0 %copy-start.5 = (s32[4]{0:T(128)S(1)}, s32[4]{0:T(128)}, u32[]{:S(2)}) copy-start(s32[4]{0:T(128)} %param.16) | copy-start | bytes 52
  105.3 18.9 %all-to-all-start.1 = ((bf16[8,64,512]{2,1,0:T(8,128)(2,1)}), bf16[8,64,512]{2,1,0:T(8,128)(2,1)S(1)}, u32[]{:S(2)}, u32[]{:S(2)}) async-start(bf16[8,64,512]{2,1,0:T(8,128)(2,1)} %reshape.215), calls=%async_computation.2 | async-start | bytes 1048576 | tf_op jit(solution)/shard_map/all_to_all | solution.py:88
  126.5 4.8 %copy-start.1 = (f32[256,128]{0,1:T(8,128)S(1)}, f32[256,128]{0,1:T(8,128)}, u32[]{:S(2)}) copy-start(f32[256,128]{0,1:T(8,128)} %get-tuple-element.26) | copy-start | bytes 393220
Sparse Core Ops, SparseCore 0:
  71.3 31.0 all-reduce.1
  105.1 24.9 reduce-scatter.1

commit v2 on v1

--- a/solution.py
+++ b/solution.py
@@ -1,8 +1,11 @@
+import functools
 import math
 
 import jax
 import jax.numpy as jnp
 from jax import lax
+from jax.experimental import pallas as pl
+from jax.experimental.pallas import tpu as pltpu
 from jax.sharding import PartitionSpec as P
 
 rope_base = 1000000.0
@@ -17,6 +20,202 @@
     angles = jnp.concatenate([angles, angles], axis=-1)
     turned = jnp.concatenate([-key_part[..., half_dim:], key_part[..., :half_dim]], axis=-1)
     return key_part * jnp.cos(angles) + turned * jnp.sin(angles)
+
+
+def other(index, distance, count):
+    total = 0
+    step = 1
+    while step < count:
+        bit = lax.rem(index // step, 2)
+        total = total + (bit if (distance // step) % 2 == 0 else 1 - bit) * step
+        step *= 2
+    return total
+
+
+def adapter_kernel(
+    dp_count,
+    tensor_count,
+    pick_ref,
+    slot_ref,
+    mine_ref,
+    tokens_ref,
+    down_ref,
+    up_ref,
+    delta_ref,
+    up_wide,
+    outgoing,
+    visiting,
+    part,
+    peer,
+    served,
+    returned,
+    token_send,
+    token_recv,
+    peer_send,
+    peer_recv,
+    delta_send,
+    delta_recv,
+):
+    me_dp = lax.axis_index("dp")
+    me_tensor = lax.axis_index("tensor")
+    stored, heads = up_ref.shape[0], up_ref.shape[1]
+    rank, half = up_ref.shape[3], up_ref.shape[4]
+    partner = [other(me_dp, j, dp_count) for j in range(dp_count)]
+    mate = [other(me_tensor, q, tensor_count) for q in range(tensor_count)]
+
+    barrier = pltpu.get_barrier_semaphore()
+    for j in range(1, dp_count):
+        pl.semaphore_signal(
+            barrier, inc=1, device_id={"dp": partner[j]}, device_id_type=pl.DeviceIdType.MESH
+        )
+    for q in range(1, tensor_count):
+        pl.semaphore_signal(
+            barrier, inc=1, device_id={"tensor": mate[q]}, device_id_type=pl.DeviceIdType.MESH
+        )
+
+    def token_copy(j):
+        return pltpu.make_async_remote_copy(
+            src_ref=outgoing.at[j - 1],
+            dst_ref=visiting.at[j - 1],
+            send_sem=token_send.at[j - 1],
+            recv_sem=token_recv.at[j - 1],
+            device_id={"dp": partner[j]},
+            device_id_type=pl.DeviceIdType.MESH,
+        )
+
+    def peer_copy(j, q):
+        return pltpu.make_async_remote_copy(
+            src_ref=part.at[j],
+            dst_ref=peer.at[j, q - 1],
+            send_sem=peer_send.at[j, q - 1],
+            recv_sem=peer_recv.at[j, q - 1],
+            device_id={"tensor": mate[q]},
+            device_id_type=pl.DeviceIdType.MESH,
+        )
+
+    def delta_copy(j):
+        return pltpu.make_async_remote_copy(
+            src_ref=served.at[j - 1],
+            dst_ref=returned.at[j],
+            send_sem=delta_send.at[j - 1],
+            recv_sem=delta_recv.at[j - 1],
+            device_id={"dp": partner[j]},
+            device_id_type=pl.DeviceIdType.MESH,
+        )
+
+    def fill(j):
+        outgoing[j - 1] = tokens_ref[pick_ref[j]]
+
+    far = list(range(dp_count - 1, dp_count // 2 - 1, -1))
+    near = list(range(dp_count // 2 - 1, 0, -1))
+    first = far[:2] + near[:1]
+    for j in first:
+        fill(j)
+    pl.semaphore_wait(barrier, dp_count + tensor_count - 2)
+    for j in first:
+        token_copy(j).start()
+    far_waiting, near_waiting = far[2:], near[1:]
+    for j in far_waiting + near_waiting:
+        fill(j)
+
+    up_wide[...] = jnp.zeros_like(up_wide)
+    for s in range(stored):
+        for h in range(heads):
+            for g in range(2):
+                at = (2 * h + g) * half
+                up_wide[s, g * rank : (g + 1) * rank, at : at + half] = up_ref[s, h, g]
+
+    def down_stage(j):
+        if j == 0:
+            rows = tokens_ref[pick_ref[0]]
+        else:
+            token_copy(j).wait_recv()
+            rows = visiting[j - 1]
+        part[j] = jnp.dot(
+            rows, down_ref[slot_ref[j]], preferred_element_type=jnp.float32
+        ).astype(jnp.bfloat16)
+        for q in range(1, tensor_count):
+            peer_copy(j, q).start()
+
+    def up_stage(j):
+        total = part[j].astype(jnp.float32)
+        for q in range(1, tensor_count):
+            peer_copy(j, q).wait_recv()
+            total = total + peer[j, q - 1].astype(jnp.float32)
+        result = jnp.dot(
+            total.astype(jnp.bfloat16), up_wide[slot_ref[j]], preferred_element_type=jnp.float32
+        ).astype(jnp.bfloat16)
+        if j == 0:
+            returned[0] = result
+        else:
+            served[j - 1] = result
+            delta_copy(j).start()
+
+    order = [0]
+    for a, b in zip(near, far[: len(near)]):
+        order += [a, b]
+    order += far[len(near) :]
+    behind = None
+    for j in order:
+        down_stage(j)
+        if j != 0:
+            waiting = far_waiting if j >= dp_count // 2 else near_waiting
+            token_copy(j).wait_send()
+            if waiting:
+                token_copy(waiting.pop(0)).start()
+        if behind is not None:
+            up_stage(behind)
+        behind = j
+    up_stage(behind)
+    for j in order:
+        if j != 0:
+            delta_copy(j).wait_recv()
+    for c in range(delta_ref.shape[0]):
+        delta_ref[c] = returned[mine_ref[c]]
+    for j in range(dp_count):
+        if j != 0:
+            delta_copy(j).wait_send()
+        for q in range(1, tensor_count):
+            peer_copy(j, q).wait_send()
+
+
+def adapter_path(conversation_rows, down, up, pick, slot, mine):
+    dp_count, tensor_count = lax.axis_size("dp"), lax.axis_size("tensor")
+    conversations, span, width = conversation_rows.shape
+    stored, _, double_rank = down.shape
+    wide = up.shape[1] * 2 * up.shape[4]
+    kind = conversation_rows.dtype
+    smem = pl.BlockSpec(memory_space=pltpu.SMEM)
+    vmem = pl.BlockSpec(memory_space=pltpu.VMEM)
+    return pl.pallas_call(
+        functools.partial(adapter_kernel, dp_count, tensor_count),
+        out_shape=jax.ShapeDtypeStruct((conversations, span, wide), kind),
+        in_specs=[smem, smem, smem, vmem, vmem, vmem],
+        out_specs=vmem,
+        scratch_shapes=[
+            pltpu.VMEM((stored, double_rank, wide), kind),
+            pltpu.VMEM((dp_count - 1, span, width), kind),
+            pltpu.VMEM((dp_count - 1, span, width), kind),
+            pltpu.VMEM((dp_count, span, double_rank), kind),
+            pltpu.VMEM((dp_count, tensor_count - 1, span, double_rank), kind),
+            pltpu.VMEM((dp_count - 1, span, wide), kind),
+            pltpu.VMEM((dp_count, span, wide), kind),
+            pltpu.SemaphoreType.DMA((dp_count - 1,)),
+            pltpu.SemaphoreType.DMA((dp_count - 1,)),
+            pltpu.SemaphoreType.DMA((dp_count, tensor_count - 1)),
+            pltpu.SemaphoreType.DMA((dp_count, tensor_count - 1)),
+            pltpu.SemaphoreType.DMA((dp_count - 1,)),
+            pltpu.SemaphoreType.DMA((dp_count - 1,)),
+        ],
+        compiler_params=pltpu.CompilerParams(
+            collective_id=0, has_side_effects=True, vmem_limit_bytes=40 * 2**20
+        ),
+        cost_estimate=pl.CostEstimate(
+            flops=2 * dp_count * span * width * double_rank,
+            bytes_accessed=60_000_000,
+            transcendentals=0,
+        ),
+    )(pick, slot, mine, conversation_rows, down, up)
 
 
 def body(
@@ -39,7 +238,6 @@
     head_span_width = key_value_bias.shape[1]
     head_dim = head_span_width // 2
     locally_stored = adapter_down_weight.shape[0]
-    double_rank = adapter_down_weight.shape[2]
     adapter_ids = jnp.arange(adapter_slot_table.shape[0], dtype=jnp.int32)
     storage = jnp.sum(
         jnp.where(
@@ -51,14 +249,18 @@
     local_table = (storage % locally_stored).reshape(dp_count, conversation_present)
     my_owners = lax.dynamic_slice_in_dim(owner_table, owner_index, 1, 0)[0]
     owner_ids = jnp.arange(dp_count, dtype=jnp.int32)
+    owner_ids = jnp.arange(dp_count, dtype=jnp.int32)
+    partner_ids = owner_index ^ owner_ids
+    conversation_ids = jnp.arange(conversation_present, dtype=jnp.int32)
+    pick = jnp.sum(
+        jnp.where(my_owners[None, :] == partner_ids[:, None], conversation_ids[None, :], 0), axis=1
+    )
     served_slot = jnp.sum(jnp.where(owner_table == owner_index, local_table, 0), axis=1)
+    slot = jnp.sum(
+        jnp.where(partner_ids[:, None] == owner_ids[None, :], served_slot[None, :], 0), axis=1
+    )
+    mine = my_owners ^ owner_index
     conversation_rows = tokens.reshape(conversation_present, span_token_rows, slice_width)
-    outgoing = jnp.zeros((dp_count, span_token_rows, slice_width), tokens.dtype)
-    for c in range(conversation_present):
-        outgoing = jnp.where(
-            (my_owners[c] == owner_ids)[:, None, None], conversation_rows[c][None], outgoing
-        )
-    visiting = lax.all_to_all(outgoing, "dp", split_axis=0, concat_axis=0, tiled=True)
     base_sum = lax.psum_scatter(
         jnp.einsum(
             "td,dhe->hte", tokens, key_value_weight, preferred_element_type=jnp.float32
@@ -67,30 +269,9 @@
         scatter_dimension=0,
         tiled=True,
     ).astype(jnp.float32)
-    rank_each = jnp.einsum(
-        "crd,sdk->scrk", visiting, adapter_down_weight, preferred_element_type=jnp.float32
-    )
-    rank_part = rank_each[0]
-    up_served = adapter_up_weight[0][None]
-    for s in range(1, locally_stored):
-        rank_part = jnp.where((served_slot == s)[:, None, None], rank_each[s], rank_part)
-        up_served = jnp.where(
-            (served_slot == s)[:, None, None, None, None], adapter_up_weight[s][None], up_served
-        )
-    rank_sum = lax.psum(rank_part.astype(jnp.bfloat16), "tensor")
-    rank_halves = rank_sum.reshape(dp_count, span_token_rows, 2, double_rank // 2)
-    served_delta = jnp.einsum(
-        "crgm,chgmf->crhgf", rank_halves, up_served, preferred_element_type=jnp.float32
-    ).astype(jnp.bfloat16)
-    served_delta = served_delta.reshape(
-        dp_count, span_token_rows, heads_present * head_span_width
-    )
-    returned = lax.all_to_all(served_delta, "dp", split_axis=0, concat_axis=0, tiled=True)
-    adapter_delta = jnp.zeros((conversation_present,) + returned.shape[1:], returned.dtype)
-    for o in range(dp_count):
-        adapter_delta = jnp.where(
-            (my_owners == o)[:, None, None], returned[o][None], adapter_delta
-        )
+    adapter_delta = adapter_path(
+        conversation_rows, adapter_down_weight, adapter_up_weight, pick, slot, mine
+    )
     conversation_delta = adapter_delta.reshape(
         conversation_present, span_token_rows, heads_present * head_span_width
     ).astype(jnp.float32)

time: 139 us -> 94.1 us (0.68)
  waiting for transfers between devices: 81.1 us -> 0.04 us
  Pallas kernels: 0 us -> 66.3 us
  starting transfers between devices: 12.9 us -> 0.04 us
  local copies, waits for them, and re-layouts: 12 us -> 1.67 us
  other arithmetic: 8.18 us -> 2.52 us
  matrix products: 11.3 us -> 9.38 us
    pallas_call x0 -> x1, Pallas kernels: none -> 66.3 us  [adapter_path(): pl.pallas_call(functools.partial(adapter_kernel, dp_count, tensor_count),...]
    all_to_all x2 -> x0, waiting for transfers between devices: 55.6 us -> none  [the longest x1 48.2 us: body(): lax.all_to_all(outgoing, 'dp', split_axis=0, concat_axis=0, tiled=True)]
    psum x1 -> x0, waiting for transfers between devices: 21.9 us -> none  [body(): rank_sum = lax.psum(rank_part.astype(jnp.bfloat16), 'tensor')]
    all_to_all x2 -> x0, starting transfers between devices: 12.8 us -> none  [the longest x1 7.25 us: body(): lax.all_to_all(outgoing, 'dp', split_axis=0, concat_axis=0, tiled=True)]
    broadcast_in_dim x42 -> x0, local copies, waits for them, and re-layouts: 6.52 us -> none  [the longest x41 6.51 us: body(): jnp.where((my_owners == o)[:, None, None], returned[o][None], adapter_delta)]
    reduce_scatter x1, waiting for transfers between devices: 3.6 us -> 0.02 us  [body(): lax.psum_scatter(jnp.einsum('td,dhe->hte', tokens, key_value_weight, pref...]
    eq x5 -> x0, other arithmetic: 2.55 us -> none  [the longest x2 2.52 us: body(): my_owners[c] == owner_ids]
    select_n x2 -> x0, other arithmetic: 2.05 us -> none  [the longest x1 1.92 us: body(): jnp.where((my_owners[c] == owner_ids)[:, None, None], conversation_rows[c...]
  transfers between devices with their start and end apart: 4 -> 1, of which waited for: 4 -> 0; matrix products, arithmetic and copies ran while one was open for 15% -> 2% of each run, Pallas kernels for 0% -> 71%
where the time goes in v2:
time: 94.1 us; the launch traced here: 93.5 us
  Pallas kernels  66.3 us (70%)
  between operations  13.6 us (14%)
  matrix products  9.38 us (10%)
  other arithmetic  2.52 us (3%)
  local copies, waits for them, and re-layouts  1.67 us (2%)
    pallas_call x1, Pallas kernels, adapter_path(): pl.pallas_call(functools.partial(adapter_kernel, dp_count, tensor_count),...  66.3 us
    dot_general x1, matrix products, body(): jnp.einsum('td,dhe->hte', tokens, key_value_weight, preferred_element_typ...  9.38 us
  transfers between devices with their start and end apart: 1, of which 0 were waited for; matrix products, arithmetic and copies ran while one was open for 2% of the time, Pallas kernels for 71%

profile of v2, /device:TPU:0, one launch (start us, length us, event | category | flops | bytes accessed | tf_op | source)
XLA Modules:
  0.0 93.5 jit_solution(3757882283700933960)
XLA Ops:
  6.5 0.0 copy-start.3
  6.6 0.0 copy-start.4
  6.6 0.0 copy-start.7
  6.6 0.0 reduce-scatter.2.cloned.1.call-start
  6.6 9.4 %fusion.5 = bf16[8,256,256]{1,2,0:T(8,128)(2,1)} fusion(bf16[2048,8,256]{2,1,0:T(8,128)(2,1)} %param.10, bf16[256,2048]{1,0:T(8,128)(2,1)} %param.9), kind=kOutput, calls=%fused_computation.3 | convolution fusion | flops 2148007936 | bytes 10485760 | tf_op jit(solution)/shard_map/td,dhe->hte/dot_general | solution.py:265
  16.0 0.0 reduce-scatter.2.cloned.1.call-update
  16.0 0.0 copy-done.6
  16.0 0.0 copy-done.5
  16.1 0.1 select_reduce_fusion
  16.1 0.1 reduce_sum.39
  16.2 0.1 fusion.14
  16.4 0.2 select_reduce_fusion.2.pick_ref
  16.5 0.2 select_reduce_fusion.1.slot_ref
  16.7 0.0 copy-done
  16.7 0.0 copy-done.1
  16.7 0.0 copy-done.2
  16.8 66.3 %shard_map.91 = bf16[4,64,512]{2,1,0:T(8,128)(2,1)S(1)} custom-call(s32[8]{0:T(128)S(1)} %select_reduce_fusion.2.pick_ref, s32[8]{0:T(128)S(1)} %select_reduce_fusion.1.slot_ref, s32[4]{0:T(128)S(1)} %get-tuple-element.5.mine_ref, bf16[4,64,2048]{2,1,0:T(8,128)(2,1)S(1)} %bitcast.11, bf16[2,2048,128]{2,1,0:T(8,128)(2,1)S(1)} %copy-done.1, ...), custom_call_target="tpu_custom_call" | custom-call | flops 268435456 | bytes 60000000 | tf_op jit(solution)/shard_map/pallas_call | solution.py:190
  83.0 0.3 reshape.110
  83.4 0.2 copy.17
  83.6 0.0 copy-done.3
  83.6 0.0 copy-done.4
  83.6 0.1 add_convert_fusion
  83.7 0.1 convert_element_type.31
  83.8 0.0 copy-done.7
  83.8 0.1 iota_compare_fusion.2
  83.8 0.1 lt.34
  83.9 0.1 broadcast_multiply_fusion
  84.0 0.5 fusion.12
  84.5 0.0 reduce-scatter.2.cloned.1.call-done
  84.5 1.1 %bitcast_add_fusion = f32[2,256,256]{1,2,0:T(8,128)S(1)} fusion(f32[256,2,256]{0,2,1:T(8,128)S(1)} %copy.17, bf16[2,256,256]{1,2,0:T(8,128)(2,1)} %reduce-scatter.2.cloned.1.call-done, f32[2,256]{1,0:T(2,128)S(1)} %convert_element_type.29), kind=kLoop, calls=%fused_computation.7 | loop fusion | flops 393216 | bytes 1312768 | tf_op jit(solution)/shard_map/add | solution.py:284
  85.6 0.1 fusion.10
  85.8 0.8 copy.18
  (11 shorter events, 0.1 us)
Async XLA Ops:
  6.5 10.2 %copy-start = (bf16[256,2048]{1,0:T(8,128)(2,1)S(1)}, bf16[256,2048]{1,0:T(8,128)(2,1)}, u32[]{:S(2)}) copy-start(bf16[256,2048]{1,0:T(8,128)(2,1)} %param.9) | copy-start | bytes 3145732
  6.5 9.5 %copy-start.6 = (s32[32]{0:T(128)S(1)}, s32[32]{0:T(128)}, u32[]{:S(2)}) copy-start(s32[32]{0:T(128)} %param.14) | copy-start | bytes 388
  6.5 9.5 %copy-start.5 = (s32[16]{0:T(128)S(1)}, s32[16]{0:T(128)}, u32[]{:S(2)}) copy-start(s32[16]{0:T(128)} %param.15) | copy-start | bytes 196
  6.5 10.2 %copy-start.1 = (bf16[2,2048,128]{2,1,0:T(8,128)(2,1)S(1)}, bf16[2,2048,128]{2,1,0:T(8,128)(2,1)}, u32[]{:S(2)}) copy-start(bf16[2,2048,128]{2,1,0:T(8,128)(2,1)} %down_ref.1) | copy-start | bytes 3145732
  6.5 10.2 %copy-start.2 = (bf16[2,2,2,64,128]{4,3,2,1,0:T(8,128)(2,1)S(1)}, bf16[2,2,2,64,128]{4,3,2,1,0:T(8,128)(2,1)}, u32[]{:S(2)}) copy-start(bf16[2,2,2,64,128]{4,3,2,1,0:T(8,128)(2,1)} %up_ref.1) | copy-start | bytes 393220
  6.5 77.0 %copy-start.3 = (bf16[2,256]{1,0:T(2,128)(2,1)S(1)}, bf16[2,256]{1,0:T(2,128)(2,1)}, u32[]{:S(2)}) copy-start(bf16[2,256]{1,0:T(2,128)(2,1)} %param.11) | copy-start | bytes 3076
  6.6 77.0 %copy-start.4 = (s32[4]{0:T(128)S(1)}, s32[4]{0:T(128)}, u32[]{:S(2)}) copy-start(s32[4]{0:T(128)} %param.17) | copy-start | bytes 52
  6.6 77.2 %copy-start.7 = (s32[4]{0:T(128)S(1)}, s32[4]{0:T(128)}, u32[]{:S(2)}) copy-start(s32[4]{0:T(128)} %param.16) | copy-start | bytes 52
  6.6 77.9 %reduce-scatter.2.cloned.1.call-start = ((), (), s32[]{:S(2)}) async-start(), calls=%async_computation.1 | async-start | bytes 1310720 | tf_op jit(solution)/shard_map/reduce_scatter | solution.py:264
Sparse Core Ops, SparseCore 0:
  16.1 27.5 reduce-scatter.1

commit v3 on v2

--- a/solution.py
+++ b/solution.py
@@ -11,15 +11,17 @@
 rope_base = 1000000.0
 
 
-def rotary(key_part, positions):
-    half_dim = key_part.shape[-1] // 2
+def rotary_tables(positions, head_dim):
+    half_dim = head_dim // 2
     inverse_freq = jnp.exp(
-        jnp.arange(half_dim, dtype=jnp.float32) * (-2.0 * math.log(rope_base) / key_part.shape[-1])
+        jnp.arange(half_dim, dtype=jnp.float32) * (-2.0 * math.log(rope_base) / head_dim)
     )
     angles = positions[:, None] * inverse_freq[None, :]
-    angles = jnp.concatenate([angles, angles], axis=-1)
-    turned = jnp.concatenate([-key_part[..., half_dim:], key_part[..., :half_dim]], axis=-1)
-    return key_part * jnp.cos(angles) + turned * jnp.sin(angles)
+    cosines, sines = jnp.cos(angles), jnp.sin(angles)
+    return (
+        jnp.concatenate([cosines, cosines], axis=-1),
+        jnp.concatenate([-sines, sines], axis=-1),
+    )
 
 
 def other(index, distance, count):
@@ -32,7 +34,7 @@
     return total
 
 
-def adapter_kernel(
+def projection_kernel(
     dp_count,
     tensor_count,
     pick_ref,
@@ -41,7 +43,17 @@
     tokens_ref,
     down_ref,
     up_ref,
-    delta_ref,
+    weight_ref,
+    bias_ref,
+    cos_ref,
+    sin_ref,
+    live_ref,
+    result_ref,
+    raw_weight,
+    head_weight,
+    base_part,
+    base_peer,
+    base_total,
     up_wide,
     outgoing,
     visiting,
@@ -55,6 +67,9 @@
     peer_recv,
     delta_send,
     delta_recv,
+    weight_sem,
+    base_send,
+    base_recv,
 ):
     me_dp = lax.axis_index("dp")
     me_tensor = lax.axis_index("tensor")
@@ -62,6 +77,21 @@
     rank, half = up_ref.shape[3], up_ref.shape[4]
     partner = [other(me_dp, j, dp_count) for j in range(dp_count)]
     mate = [other(me_tensor, q, tensor_count) for q in range(tensor_count)]
+
+    chunks = weight_sem.shape[0]
+    chunk = weight_ref.shape[0] // chunks
+    conversations, span = tokens_ref.shape[0], tokens_ref.shape[1]
+    width = tokens_ref.shape[2]
+
+    def weight_copy(n):
+        return pltpu.make_async_copy(
+            weight_ref.at[pl.ds(n * chunk, chunk)],
+            raw_weight.at[pl.ds(n * chunk, chunk)],
+            weight_sem.at[n],
+        )
+
+    for n in range(chunks):
+        weight_copy(n).start()
 
     barrier = pltpu.get_barrier_semaphore()
     for j in range(1, dp_count):
@@ -103,18 +133,52 @@
             device_id_type=pl.DeviceIdType.MESH,
         )
 
+    def base_copy(q):
+        return pltpu.make_async_remote_copy(
+            src_ref=base_part.at[q],
+            dst_ref=base_peer.at[q - 1],
+            send_sem=base_send.at[q - 1],
+            recv_sem=base_recv.at[q - 1],
+            device_id={"tensor": mate[q]},
+            device_id_type=pl.DeviceIdType.MESH,
+        )
+
+    def turn_weight(n):
+        weight_copy(n).wait()
+        block = raw_weight[n * chunk : (n + 1) * chunk]
+        for h in range(block.shape[1]):
+            head_weight[h, n * chunk : (n + 1) * chunk] = block[:, h, :]
+
+    def base_stage(q):
+        rows = tokens_ref[...].reshape(conversations * span, width)
+        for h in range(heads):
+            base_part[q, h] = jnp.dot(
+                rows, head_weight[mate[q] * heads + h], preferred_element_type=jnp.float32
+            ).astype(jnp.bfloat16)
+        if q != 0:
+            base_copy(q).start()
+
+    def base_finish():
+        for q in range(1, tensor_count):
+            base_copy(q).wait_recv()
+        for h in range(heads):
+            total = base_part[0, h].astype(jnp.float32)
+            for q in range(1, tensor_count):
+                total = total + base_peer[q - 1, h].astype(jnp.float32)
+            base_total[h] = total + bias_ref[h : h + 1, :].astype(jnp.float32)
+
     def fill(j):
         outgoing[j - 1] = tokens_ref[pick_ref[j]]
 
     far = list(range(dp_count - 1, dp_count // 2 - 1, -1))
     near = list(range(dp_count // 2 - 1, 0, -1))
-    first = far[:2] + near[:1]
+    first = [far[0], near[0], far[1], near[1], far[2]]
     for j in first:
         fill(j)
     pl.semaphore_wait(barrier, dp_count + tensor_count - 2)
     for j in first:
         token_copy(j).start()
-    far_waiting, near_waiting = far[2:], near[1:]
+    far_waiting, near_waiting = far[3:], near[2:]
     for j in far_waiting + near_waiting:
         fill(j)
 
@@ -155,44 +219,72 @@
     for a, b in zip(near, far[: len(near)]):
         order += [a, b]
     order += far[len(near) :]
-    behind = None
-    for j in order:
+    down_stage(0)
+    for n in range(chunks):
+        turn_weight(n)
+    base_stages = list(range(1, tensor_count)) + [0]
+    base_stages = [base_stages[n::3] for n in range(3)]
+    order = order[1:]
+    behind = 0
+    for n, j in enumerate(order):
         down_stage(j)
         if j != 0:
             waiting = far_waiting if j >= dp_count // 2 else near_waiting
             token_copy(j).wait_send()
             if waiting:
                 token_copy(waiting.pop(0)).start()
-        if behind is not None:
-            up_stage(behind)
+        if n < 3:
+            for q in base_stages[n]:
+                base_stage(q)
+        up_stage(behind)
+        if n == 4:
+            base_finish()
         behind = j
     up_stage(behind)
     for j in order:
-        if j != 0:
-            delta_copy(j).wait_recv()
-    for c in range(delta_ref.shape[0]):
-        delta_ref[c] = returned[mine_ref[c]]
+        delta_copy(j).wait_recv()
+    for c in range(conversations):
+        delta = returned[mine_ref[c]].astype(jnp.float32)
+        at = slice(c * span, (c + 1) * span)
+        for h in range(heads):
+            whole = base_total[h, at, :] + delta[:, 2 * half * h : 2 * half * (h + 1)]
+            key_part, value_part = whole[:, :half], whole[:, half:]
+            turned = pltpu.roll(key_part, half // 2, 1)
+            key_part = key_part * cos_ref[at, :] + turned * sin_ref[at, :]
+            live = live_ref[at, :] > 0.5
+            result_ref[h, at, :half] = jnp.where(live, key_part, 0.0).astype(jnp.bfloat16)
+            result_ref[h, at, half:] = jnp.where(live, value_part, 0.0).astype(jnp.bfloat16)
     for j in range(dp_count):
         if j != 0:
             delta_copy(j).wait_send()
         for q in range(1, tensor_count):
             peer_copy(j, q).wait_send()
-
-
-def adapter_path(conversation_rows, down, up, pick, slot, mine):
+    for q in range(1, tensor_count):
+        base_copy(q).wait_send()
+
+
+def project(conversation_rows, down, up, weight, bias, cosines, sines, live, pick, slot, mine):
     dp_count, tensor_count = lax.axis_size("dp"), lax.axis_size("tensor")
     conversations, span, width = conversation_rows.shape
     stored, _, double_rank = down.shape
     wide = up.shape[1] * 2 * up.shape[4]
     kind = conversation_rows.dtype
+    heads, head_width = bias.shape
+    rows = conversations * span
+    chunks = 8
     smem = pl.BlockSpec(memory_space=pltpu.SMEM)
     vmem = pl.BlockSpec(memory_space=pltpu.VMEM)
     return pl.pallas_call(
-        functools.partial(adapter_kernel, dp_count, tensor_count),
-        out_shape=jax.ShapeDtypeStruct((conversations, span, wide), kind),
-        in_specs=[smem, smem, smem, vmem, vmem, vmem],
+        functools.partial(projection_kernel, dp_count, tensor_count),
+        out_shape=jax.ShapeDtypeStruct((heads, rows, head_width), kind),
+        in_specs=[smem] * 3 + [vmem] * 3 + [pl.BlockSpec(memory_space=pl.ANY)] + [vmem] * 4,
         out_specs=vmem,
         scratch_shapes=[
+            pltpu.VMEM(weight.shape, kind),
+            pltpu.VMEM((weight.shape[1], width, head_width), kind),
+            pltpu.VMEM((tensor_count, heads, rows, head_width), kind),
+            pltpu.VMEM((tensor_count - 1, heads, rows, head_width), kind),
+            pltpu.VMEM((heads, rows, head_width), jnp.float32),
             pltpu.VMEM((stored, double_rank, wide), kind),
             pltpu.VMEM((dp_count - 1, span, width), kind),
             pltpu.VMEM((dp_count - 1, span, width), kind),
@@ -206,16 +298,19 @@
             pltpu.SemaphoreType.DMA((dp_count, tensor_count - 1)),
             pltpu.SemaphoreType.DMA((dp_count - 1,)),
             pltpu.SemaphoreType.DMA((dp_count - 1,)),
+            pltpu.SemaphoreType.DMA((chunks,)),
+            pltpu.SemaphoreType.DMA((tensor_count - 1,)),
+            pltpu.SemaphoreType.DMA((tensor_count - 1,)),
         ],
         compiler_params=pltpu.CompilerParams(
-            collective_id=0, has_side_effects=True, vmem_limit_bytes=40 * 2**20
+            collective_id=0, has_side_effects=True, vmem_limit_bytes=52 * 2**20
         ),
         cost_estimate=pl.CostEstimate(
             flops=2 * dp_count * span * width * double_rank,
             bytes_accessed=60_000_000,
             transcendentals=0,
         ),
-    )(pick, slot, mine, conversation_rows, down, up)
+    )(pick, slot, mine, conversation_rows, down, up, weight, bias, cosines, sines, live)
 
 
 def body(
@@ -234,7 +329,6 @@
     conversation_present = span_length.shape[0]
     span_token_rows = tokens.shape[0] // conversation_present
     slice_width = tokens.shape[1]
-    heads_present = key_value_bias.shape[0]
     head_span_width = key_value_bias.shape[1]
     head_dim = head_span_width // 2
     locally_stored = adapter_down_weight.shape[0]
@@ -261,38 +355,31 @@
     )
     mine = my_owners ^ owner_index
     conversation_rows = tokens.reshape(conversation_present, span_token_rows, slice_width)
-    base_sum = lax.psum_scatter(
-        jnp.einsum(
-            "td,dhe->hte", tokens, key_value_weight, preferred_element_type=jnp.float32
-        ).astype(jnp.bfloat16),
-        "tensor",
-        scatter_dimension=0,
-        tiled=True,
-    ).astype(jnp.float32)
-    adapter_delta = adapter_path(
-        conversation_rows, adapter_down_weight, adapter_up_weight, pick, slot, mine
-    )
-    conversation_delta = adapter_delta.reshape(
-        conversation_present, span_token_rows, heads_present * head_span_width
-    ).astype(jnp.float32)
-    delta_heads = jnp.transpose(
-        conversation_delta.reshape(
-            conversation_present * span_token_rows, heads_present, head_span_width
-        ),
-        (1, 0, 2),
-    )
-    projected = base_sum + key_value_bias.astype(jnp.float32)[:, None, :] + delta_heads
     positions = (
         (context_length[:, None] + jnp.arange(span_token_rows, dtype=jnp.int32)[None, :])
         .reshape(-1)
         .astype(jnp.float32)
     )
-    rotated = rotary(projected[..., :head_dim], positions)
+    cosines, sines = rotary_tables(positions, head_dim)
     live_mask = (
         jnp.arange(span_token_rows, dtype=jnp.int32)[None, :] < span_length[:, None]
     ).reshape(-1)
-    joined = jnp.concatenate([rotated, projected[..., head_dim:]], axis=-1)
-    return jnp.where(live_mask[None, :, None], joined, 0.0).astype(jnp.bfloat16)
+    live = jnp.broadcast_to(
+        live_mask[:, None].astype(jnp.float32), (live_mask.shape[0], head_dim)
+    )
+    return project(
+        conversation_rows,
+        adapter_down_weight,
+        adapter_up_weight,
+        key_value_weight,
+        key_value_bias,
+        cosines,
+        sines,
+        live,
+        pick,
+        slot,
+        mine,
+    )
 
 
 def solution(mesh):

time: 94.1 us -> 73.9 us (0.79)
  between operations: 13.6 us -> 0.06 us
  matrix products: 9.38 us -> 0 us
  local copies, waits for them, and re-layouts: 1.67 us -> 3.85 us
    dot_general x1 -> x0, matrix products: 9.38 us -> none  [body(): jnp.einsum('td,dhe->hte', tokens, key_value_weight, preferred_element_typ...]
    unnamed x16 -> x7, local copies, waits for them, and re-layouts: 0.03 us -> 3.51 us
    add x2 -> x0, other arithmetic: 1.16 us -> none  [the longest x1 1.09 us: body(): base_sum + key_value_bias.astype(jnp.float32)[:, None, :] + delta_heads]
  transfers between devices with their start and end apart: 1 -> 0, of which waited for: 0 -> 0; matrix products, arithmetic and copies ran while one was open for 2% -> 0% of each run, Pallas kernels for 71% -> 0%
where the time goes in v3:
time: 73.9 us; the launch traced here: 73.7 us
  Pallas kernels  66.4 us (90%)
  local copies, waits for them, and re-layouts  3.85 us (5%)
  other arithmetic  3.4 us (5%)
    pallas_call x1, Pallas kernels, project(): pl.pallas_call(functools.partial(projection_kernel, dp_count, tensor_coun...  66.4 us
    unnamed x7, local copies, waits for them, and re-layouts  3.51 us

profile of v3, /device:TPU:0, one launch (start us, length us, event | category | flops | bytes accessed | tf_op | source)
XLA Modules:
  0.0 73.7 jit_solution(11411085758155067843)
XLA Ops:
  0.0 0.8 %select_reduce_fusion = s32[32]{0:T(128)S(1)} fusion(s32[16]{0:T(128)} %param.15, s32[32]{0:T(128)} %param.14), kind=kLoop, calls=%fused_computation.5 | loop fusion | flops 1504 | bytes 320 | tf_op jit(solution)/shard_map/reduce_sum | solution.py:336
  0.8 0.1 reduce_sum.39
  0.8 0.1 fusion.2
  1.0 0.2 select_reduce_fusion.2.pick_ref
  1.2 0.2 select_reduce_fusion.1.slot_ref
  1.4 0.7 add_convert_fusion
  2.1 0.1 convert_element_type.22
  2.2 0.5 fusion
  2.7 0.1 pad_maximum_fusion
  2.9 0.7 fusion.5
  3.6 0.1 reshape.54
  3.7 0.1 broadcast_in_dim.60.live_ref
  3.8 0.0 copy-start
  3.8 1.2 %copy-done = bf16[256,2048]{1,0:T(8,128)(2,1)S(1)} copy-done((bf16[256,2048]{1,0:T(8,128)(2,1)S(1)}, bf16[256,2048]{1,0:T(8,128)(2,1)}, u32[]{:S(2)}) %copy-start) | copy-done | bytes 1048600
  5.0 0.0 copy-start.1
  5.0 0.9 %copy-done.1 = bf16[2,2,2,64,128]{4,3,2,1,0:T(8,128)(2,1)S(1)} copy-done((bf16[2,2,2,64,128]{4,3,2,1,0:T(8,128)(2,1)S(1)}, bf16[2,2,2,64,128]{4,3,2,1,0:T(8,128)(2,1)}, u32[]{:S(2)}) %copy-start.1) | copy-done | bytes 131096
  5.9 0.0 copy-start.2
  5.9 0.7 copy-done.2
  6.6 66.4 %shard_map.91 = bf16[2,256,256]{2,1,0:T(8,128)(2,1)S(1)} custom-call(s32[8]{0:T(128)S(1)} %select_reduce_fusion.2.pick_ref, s32[8]{0:T(128)S(1)} %select_reduce_fusion.1.slot_ref, s32[4]{0:T(128)S(1)} %get-tuple-element.5.mine_ref, bf16[4,64,2048]{2,1,0:T(8,128)(2,1)S(1)} %bitcast.4, bf16[2,2048,128]{2,1,0:T(8,128)(2,1)} %down_ref.1, ...), custom_call_target="tpu_custom_call" | custom-call | flops 268435456 | bytes 60000000 | tf_op jit(solution)/shard_map/pallas_call | solution.py:277
  73.0 0.7 copy.11
  (3 shorter events, 0.0 us)
Async XLA Ops:
  3.8 1.2 %copy-start = (bf16[256,2048]{1,0:T(8,128)(2,1)S(1)}, bf16[256,2048]{1,0:T(8,128)(2,1)}, u32[]{:S(2)}) copy-start(bf16[256,2048]{1,0:T(8,128)(2,1)} %param.9) | copy-start | bytes 3145732
  5.0 0.9 %copy-start.1 = (bf16[2,2,2,64,128]{4,3,2,1,0:T(8,128)(2,1)S(1)}, bf16[2,2,2,64,128]{4,3,2,1,0:T(8,128)(2,1)}, u32[]{:S(2)}) copy-start(bf16[2,2,2,64,128]{4,3,2,1,0:T(8,128)(2,1)} %up_ref.1) | copy-start | bytes 393220
  5.9 0.7 copy-start.2

commit v4 on v3

--- a/solution.py
+++ b/solution.py
@@ -40,8 +40,9 @@
     pick_ref,
     slot_ref,
     mine_ref,
+    home_ref,
     tokens_ref,
-    down_ref,
+    stored_down,
     up_ref,
     weight_ref,
     bias_ref,
@@ -54,7 +55,9 @@
     base_part,
     base_peer,
     base_total,
+    down_ref,
     up_wide,
+    up_all,
     outgoing,
     visiting,
     part,
@@ -65,15 +68,19 @@
     token_recv,
     peer_send,
     peer_recv,
-    delta_send,
-    delta_recv,
+    rank_send,
+    rank_recv,
     weight_sem,
     base_send,
     base_recv,
+    up_send,
+    up_recv,
+    down_sem,
 ):
     me_dp = lax.axis_index("dp")
     me_tensor = lax.axis_index("tensor")
-    stored, heads = up_ref.shape[0], up_ref.shape[1]
+    heads = up_ref.shape[1]
+    across = dp_count // 2
     rank, half = up_ref.shape[3], up_ref.shape[4]
     partner = [other(me_dp, j, dp_count) for j in range(dp_count)]
     mate = [other(me_tensor, q, tensor_count) for q in range(tensor_count)]
@@ -90,6 +97,8 @@
             weight_sem.at[n],
         )
 
+    down_fetch = pltpu.make_async_copy(stored_down, down_ref, down_sem)
+    down_fetch.start()
     for n in range(chunks):
         weight_copy(n).start()
 
@@ -123,12 +132,28 @@
             device_id_type=pl.DeviceIdType.MESH,
         )
 
-    def delta_copy(j):
+    def up_copy(source, j, to):
+        return pltpu.make_async_remote_copy(
+            src_ref=source,
+            dst_ref=up_all.at[j],
+            send_sem=up_send.at[j - 1],
+            recv_sem=up_recv.at[j - 1],
+            device_id={"dp": partner[to]},
+            device_id_type=pl.DeviceIdType.MESH,
+        )
+
+    def up_direct(j):
+        return up_copy(up_ref, j, j)
+
+    def up_relay(j):
+        return up_copy(up_all.at[across], across + j, j)
+
+    def rank_copy(j):
         return pltpu.make_async_remote_copy(
             src_ref=served.at[j - 1],
             dst_ref=returned.at[j],
-            send_sem=delta_send.at[j - 1],
-            recv_sem=delta_recv.at[j - 1],
+            send_sem=rank_send.at[j - 1],
+            recv_sem=rank_recv.at[j - 1],
             device_id={"dp": partner[j]},
             device_id_type=pl.DeviceIdType.MESH,
         )
@@ -182,12 +207,27 @@
     for j in far_waiting + near_waiting:
         fill(j)
 
+    for j in [across] + list(range(1, across)):
+        up_direct(j).start()
+    up_all[0] = up_ref[...]
     up_wide[...] = jnp.zeros_like(up_wide)
-    for s in range(stored):
-        for h in range(heads):
-            for g in range(2):
-                at = (2 * h + g) * half
-                up_wide[s, g * rank : (g + 1) * rank, at : at + half] = up_ref[s, h, g]
+
+    def relay_up():
+        up_direct(across).wait_recv()
+        for j in range(1, across):
+            up_relay(j).start()
+
+    def widen_up():
+        for j in range(1, across):
+            up_direct(j).wait_recv()
+            up_relay(j).wait_recv()
+        for c in range(conversations):
+            for h in range(heads):
+                for g in range(2):
+                    at = (2 * h + g) * half
+                    up_wide[c, g * rank : (g + 1) * rank, at : at + half] = up_all[
+                        mine_ref[c], home_ref[c], h, g
+                    ]
 
     def down_stage(j):
         if j == 0:
@@ -201,24 +241,23 @@
         for q in range(1, tensor_count):
             peer_copy(j, q).start()
 
-    def up_stage(j):
+    def sum_stage(j):
         total = part[j].astype(jnp.float32)
         for q in range(1, tensor_count):
             peer_copy(j, q).wait_recv()
             total = total + peer[j, q - 1].astype(jnp.float32)
-        result = jnp.dot(
-            total.astype(jnp.bfloat16), up_wide[slot_ref[j]], preferred_element_type=jnp.float32
-        ).astype(jnp.bfloat16)
+        result = total.astype(jnp.bfloat16)
         if j == 0:
             returned[0] = result
         else:
             served[j - 1] = result
-            delta_copy(j).start()
+            rank_copy(j).start()
 
     order = [0]
     for a, b in zip(near, far[: len(near)]):
         order += [a, b]
     order += far[len(near) :]
+    down_fetch.wait()
     down_stage(0)
     for n in range(chunks):
         turn_weight(n)
@@ -236,15 +275,22 @@
         if n < 3:
             for q in base_stages[n]:
                 base_stage(q)
-        up_stage(behind)
+        sum_stage(behind)
+        if n == 1:
+            relay_up()
         if n == 4:
             base_finish()
+        if n == 5:
+            widen_up()
         behind = j
-    up_stage(behind)
+    sum_stage(behind)
     for j in order:
-        delta_copy(j).wait_recv()
+        rank_copy(j).wait_recv()
     for c in range(conversations):
-        delta = returned[mine_ref[c]].astype(jnp.float32)
+        delta = jnp.dot(
+            returned[mine_ref[c]], up_wide[c], preferred_element_type=jnp.float32
+        )
+        delta = delta.astype(jnp.bfloat16).astype(jnp.float32)
         at = slice(c * span, (c + 1) * span)
         for h in range(heads):
             whole = base_total[h, at, :] + delta[:, 2 * half * h : 2 * half * (h + 1)]
@@ -256,17 +302,21 @@
             result_ref[h, at, half:] = jnp.where(live, value_part, 0.0).astype(jnp.bfloat16)
     for j in range(dp_count):
         if j != 0:
-            delta_copy(j).wait_send()
+            rank_copy(j).wait_send()
         for q in range(1, tensor_count):
             peer_copy(j, q).wait_send()
     for q in range(1, tensor_count):
         base_copy(q).wait_send()
-
-
-def project(conversation_rows, down, up, weight, bias, cosines, sines, live, pick, slot, mine):
+    for j in range(1, across + 1):
+        up_direct(j).wait_send()
+    for j in range(1, across):
+        up_relay(j).wait_send()
+
+
+def project(conversation_rows, down, up, weight, bias, cosines, sines, live, pick, slot, mine, home):
     dp_count, tensor_count = lax.axis_size("dp"), lax.axis_size("tensor")
     conversations, span, width = conversation_rows.shape
-    stored, _, double_rank = down.shape
+    double_rank = down.shape[2]
     wide = up.shape[1] * 2 * up.shape[4]
     kind = conversation_rows.dtype
     heads, head_width = bias.shape
@@ -274,10 +324,11 @@
     chunks = 8
     smem = pl.BlockSpec(memory_space=pltpu.SMEM)
     vmem = pl.BlockSpec(memory_space=pltpu.VMEM)
+    hbm = pl.BlockSpec(memory_space=pl.ANY)
     return pl.pallas_call(
         functools.partial(projection_kernel, dp_count, tensor_count),
         out_shape=jax.ShapeDtypeStruct((heads, rows, head_width), kind),
-        in_specs=[smem] * 3 + [vmem] * 3 + [pl.BlockSpec(memory_space=pl.ANY)] + [vmem] * 4,
+        in_specs=[smem] * 4 + [vmem, hbm, vmem, hbm] + [vmem] * 4,
         out_specs=vmem,
         scratch_shapes=[
             pltpu.VMEM(weight.shape, kind),
@@ -285,13 +336,15 @@
             pltpu.VMEM((tensor_count, heads, rows, head_width), kind),
             pltpu.VMEM((tensor_count - 1, heads, rows, head_width), kind),
             pltpu.VMEM((heads, rows, head_width), jnp.float32),
-            pltpu.VMEM((stored, double_rank, wide), kind),
+            pltpu.VMEM(down.shape, kind),
+            pltpu.VMEM((conversations, double_rank, wide), kind),
+            pltpu.VMEM((dp_count,) + up.shape, kind),
             pltpu.VMEM((dp_count - 1, span, width), kind),
             pltpu.VMEM((dp_count - 1, span, width), kind),
             pltpu.VMEM((dp_count, span, double_rank), kind),
             pltpu.VMEM((dp_count, tensor_count - 1, span, double_rank), kind),
-            pltpu.VMEM((dp_count - 1, span, wide), kind),
-            pltpu.VMEM((dp_count, span, wide), kind),
+            pltpu.VMEM((dp_count - 1, span, double_rank), kind),
+            pltpu.VMEM((dp_count, span, double_rank), kind),
             pltpu.SemaphoreType.DMA((dp_count - 1,)),
             pltpu.SemaphoreType.DMA((dp_count - 1,)),
             pltpu.SemaphoreType.DMA((dp_count, tensor_count - 1)),
@@ -301,6 +354,9 @@
             pltpu.SemaphoreType.DMA((chunks,)),
             pltpu.SemaphoreType.DMA((tensor_count - 1,)),
             pltpu.SemaphoreType.DMA((tensor_count - 1,)),
+            pltpu.SemaphoreType.DMA((dp_count - 1,)),
+            pltpu.SemaphoreType.DMA((dp_count - 1,)),
+            pltpu.SemaphoreType.DMA,
         ],
         compiler_params=pltpu.CompilerParams(
             collective_id=0, has_side_effects=True, vmem_limit_bytes=52 * 2**20
@@ -310,7 +366,7 @@
             bytes_accessed=60_000_000,
             transcendentals=0,
         ),
-    )(pick, slot, mine, conversation_rows, down, up, weight, bias, cosines, sines, live)
+    )(pick, slot, mine, home, conversation_rows, down, up, weight, bias, cosines, sines, live)
 
 
 def body(
@@ -354,6 +410,7 @@
         jnp.where(partner_ids[:, None] == owner_ids[None, :], served_slot[None, :], 0), axis=1
     )
     mine = my_owners ^ owner_index
+    home = lax.dynamic_slice_in_dim(local_table, owner_index, 1, 0)[0]
     conversation_rows = tokens.reshape(conversation_present, span_token_rows, slice_width)
     positions = (
         (context_length[:, None] + jnp.arange(span_token_rows, dtype=jnp.int32)[None, :])
@@ -379,6 +436,7 @@
         pick,
         slot,
         mine,
+        home,
     )
 
 

time: 73.9 us -> 78 us (1.055)
  Pallas kernels: 66.4 us -> 70 us
    pallas_call x1, Pallas kernels: 66.4 us -> 70 us  [project(): pl.pallas_call(functools.partial(projection_kernel, dp_count, tensor_coun...]
where the time goes in v4:
time: 78 us; the launch traced here: 77.3 us
  Pallas kernels  70 us (90%)
  local copies, waits for them, and re-layouts  3.85 us (5%)
  other arithmetic  3.4 us (4%)
    pallas_call x1, Pallas kernels, project(): pl.pallas_call(functools.partial(projection_kernel, dp_count, tensor_coun...  70 us
    unnamed x7, local copies, waits for them, and re-layouts  3.51 us

profile of v4, /device:TPU:0, one launch (start us, length us, event | category | flops | bytes accessed | tf_op | source)
XLA Modules:
  0.0 77.3 jit_solution(10992796584454910220)
XLA Ops:
  0.0 0.8 select_reduce_fusion
  0.8 0.1 reduce_sum.39
  0.8 0.1 add_select_fusion
  1.0 0.2 select_reduce_fusion.3.pick_ref
  1.2 0.2 select_reduce_fusion.1.slot_ref
  1.4 0.7 add_convert_fusion
  2.1 0.1 convert_element_type.22
  2.2 0.5 fusion
  2.7 0.1 pad_maximum_fusion
  2.9 0.7 fusion.3
  3.6 0.1 reshape.54
  3.7 0.1 broadcast_in_dim.60.live_ref
  3.8 0.0 copy-start
  3.8 1.2 %copy-done = bf16[256,2048]{1,0:T(8,128)(2,1)S(1)} copy-done((bf16[256,2048]{1,0:T(8,128)(2,1)S(1)}, bf16[256,2048]{1,0:T(8,128)(2,1)}, u32[]{:S(2)}) %copy-start) | copy-done | bytes 1048600
  5.0 0.0 copy-start.1
  5.0 0.9 %copy-done.1 = bf16[2,2,2,64,128]{4,3,2,1,0:T(8,128)(2,1)S(1)} copy-done((bf16[2,2,2,64,128]{4,3,2,1,0:T(8,128)(2,1)S(1)}, bf16[2,2,2,64,128]{4,3,2,1,0:T(8,128)(2,1)}, u32[]{:S(2)}) %copy-start.1) | copy-done | bytes 131096
  5.9 0.0 copy-start.2
  5.9 0.7 copy-done.2
  6.6 70.0 %shard_map.91 = bf16[2,256,256]{2,1,0:T(8,128)(2,1)S(1)} custom-call(s32[8]{0:T(128)S(1)} %select_reduce_fusion.3.pick_ref, s32[8]{0:T(128)S(1)} %select_reduce_fusion.1.slot_ref, s32[4]{0:T(128)S(1)} %get-tuple-element.5.mine_ref, s32[4]{0:T(128)S(1)} %dynamic-slice_bitcast_fusion.home_ref, bf16[4,64,2048]{2,1,0:T(8,128)(2,1)S(1)} %bitcast.6, ...), custom_call_target="tpu_custom_call" | custom-call | flops 268435456 | bytes 60000000 | tf_op jit(solution)/shard_map/pallas_call | solution.py:328
  76.6 0.7 copy.11
  (4 shorter events, 0.0 us)
Async XLA Ops:
  3.8 1.2 %copy-start = (bf16[256,2048]{1,0:T(8,128)(2,1)S(1)}, bf16[256,2048]{1,0:T(8,128)(2,1)}, u32[]{:S(2)}) copy-start(bf16[256,2048]{1,0:T(8,128)(2,1)} %param.9) | copy-start | bytes 3145732
  5.0 0.9 %copy-start.1 = (bf16[2,2,2,64,128]{4,3,2,1,0:T(8,128)(2,1)S(1)}, bf16[2,2,2,64,128]{4,3,2,1,0:T(8,128)(2,1)}, u32[]{:S(2)}) copy-start(bf16[2,2,2,64,128]{4,3,2,1,0:T(8,128)(2,1)} %up_ref.1) | copy-start | bytes 393220
  5.9 0.7 copy-start.2
